TPU v7x, 32 devices: a whole 2x2x4 slice. The times are simulated.
32 devices in a mesh: grp: 2 (over y), chan: 4 (over z), tm: 2 (over x), sub: 2 (over core).
Axes of the slice: x: 2, y: 2, z: 4, core: 2. Of those that a mesh axis runs over, the one named last changes fastest.
Arguments:
- traces: bfloat16 [1024, 4, 4096], P(('grp', 'chan'), 'tm'), parts along dimension 0
- valid: int32 [1024, 4], P(('grp', 'chan'), 'tm'), parts along dimension 0, may hold values from 0 to 1
- source_channel_index: int32 [8, 32], P(('grp', 'sub')), parts along dimension 0, may hold values from 0 to 511, as said below
Outputs:
- stack: float32 [32, 256, 512], P(None, ('grp', 'sub'), ('chan', 'tm')), parts along dimension 1
There are 2 independent parts, one for each index of `grp`. A program takes and returns all parts, laid end to end along the dimension named above; each array names one. Nothing has to cross between parts.
Inputs may be any that keep to these rules, and one draw needn't show every extreme that they name: `source_channel_index`: the 32 channels of one panel are distinct and lie in one block of 128 channels (b * 128 to b * 128 + 127); different panels lie in different blocks.
All inputs are finite; a program needn't handle non-finite values.
Results may differ from a plain program's by a relative error of at most 0.0003.
Values may be sent and summed in bfloat16 or wider, within the bound.
A program may use at most 64 MiB of HBM per device.

v0:
```python
import math
import jax
import jax.numpy as jnp
from jax import lax
from jax.sharding import PartitionSpec as P

LAGS = 32


def from_root(array, axis, root):
    mine = lax.axis_index(axis) == root
    return lax.psum(jnp.where(mine, array, jnp.zeros_like(array)), axis)


def shifted_block(src, first, count):
    width = src.shape[-1]
    rows = []
    for lag in range(first, first + count):
        rows.append(jnp.pad(src, ((0, 0), (0, 0), (lag, 0)))[:, :, :width])
    return jnp.stack(rows)


def body(traces, valid, source_channel_index):
    resident_traces = traces.shape[0]
    seg_here = traces.shape[1]
    width = traces.shape[2]
    panels_here = source_channel_index.shape[0]
    per_panel = source_channel_index.shape[1]
    rms_rec = jnp.sqrt(jnp.mean(jnp.square(traces.astype(jnp.float32)), axis=2) + 1e-05)
    rec_mask = valid.astype(jnp.float32)
    owners = source_channel_index[:, 0] // resident_traces
    local_rows = (source_channel_index - owners[:, None] * resident_traces).reshape(-1)
    picked = traces[local_rows].reshape(panels_here, per_panel, seg_here, width)
    pick_mask = valid[local_rows].reshape(panels_here, per_panel, seg_here).astype(jnp.bfloat16)

    def fetch(panel):
        return (
            from_root(picked[panel], "chan", owners[panel]),
            from_root(pick_mask[panel], "chan", owners[panel]),
        )

    fetched = [fetch(panel) for panel in range(panels_here)]
    sources = jnp.stack([item[0] for item in fetched])
    src_flags = jnp.stack([item[1] for item in fetched])
    sources = sources.reshape(panels_here * per_panel, seg_here, width)
    src_mask = src_flags.reshape(panels_here * per_panel, seg_here).astype(jnp.float32)
    rms_src = jnp.sqrt(jnp.mean(jnp.square(sources.astype(jnp.float32)), axis=2) + 1e-05)
    scale = (
        src_mask.T[:, :, None]
        * rec_mask.T[:, None, :]
        / (math.sqrt(width) * rms_src.T[:, :, None] * rms_rec.T[:, None, :])
    )
    group = min(8, LAGS)
    blocks = []
    for start in range(0, LAGS, group):
        lag_shifted = shifted_block(sources, start, group)
        lagged_product = jnp.einsum(
            "lsku,rku->klsr", lag_shifted, traces, preferred_element_type=jnp.float32
        )
        blocks.append(jnp.sum(lagged_product * scale[:, None], axis=0))
    partial_stack_value = jnp.concatenate(blocks, axis=0)
    pair_terms = jnp.dot(src_mask, rec_mask.T, preferred_element_type=jnp.float32)
    total, pairs = (
        lax.psum_scatter(partial_stack_value, "tm", scatter_dimension=2, tiled=True),
        lax.psum_scatter(pair_terms, "tm", scatter_dimension=1, tiled=True),
    )
    return total / jnp.sqrt(jnp.maximum(pairs, 1.0))[None]


def solution(mesh):
    in_specs = (P(("grp", "chan"), "tm", None), P(("grp", "chan"), "tm"), P(("grp", "sub"), None))
    out_specs = P(None, ("grp", "sub"), ("chan", "tm"))
    return jax.shard_map(body, mesh=mesh, in_specs=in_specs, out_specs=out_specs, check_vma=False)
```

profile of v0, /device:TPU:0, one launch (start us, length us, event | category | flops | bytes accessed | tf_op | source)
XLA Modules:
  0.0 146.2 jit_solution(13206774797702084006)
XLA Ops:
  7.4 0.8 multiply_reduce_fusion.2
  8.2 0.8 broadcast_subtract_fusion
  9.1 0.6 fusion.113
  11.0 4.2 %gather_fusion = bf16[64,2,4096]{2,1,0:T(2,128)(2,1)S(1)} fusion(bf16[128,2,4096]{2,1,0:T(2,128)(2,1)} %param.3, s32[1024]{0:T(1024)S(1)} %pad_clamp_fusion), kind=kCustom, calls=%fused_computation | custom fusion | bytes 2097408 | tf_op jit(solution)/shard_map/gather | solution.py:33
  15.3 1.8 %fusion.110 = (bf16[1,32,2,4096]{3,2,1,0:T(2,128)(2,1)}, bf16[1,32,2,4096]{3,2,1,0:T(2,128)(2,1)}) fusion(pred[]{:T(512)S(6)} %eq.9, bf16[64,2,4096]{2,1,0:T(2,128)(2,1)S(1)} %gather_fusion, pred[]{:T(512)S(6)} %eq.8), kind=kLoop, calls=%fused_computation.122 | loop fusion | flops 524288 | bytes 2097154 | tf_op jit(solution)/shard_map/stack | solution.py:43
  17.2 0.8 copy.53
  18.0 0.6 gather_fusion.1
  18.6 0.1 copy.54
  18.7 0.1 copy.55
  18.8 13.6 %all-reduce.31 = (bf16[1,32,2]{1,2,0:T(2,128)(2,1)S(1)}, bf16[1,32,2]{1,2,0:T(2,128)(2,1)S(1)}) all-reduce(bf16[1,32,2]{1,2,0:T(2,128)(2,1)S(1)} %bitcast.200, bf16[1,32,2]{1,2,0:T(2,128)(2,1)S(1)} %bitcast.199), channel_id=1, replica_groups=mesh['grp'=2,'chan'=4,'tm'=2,'sub'=2] {'chan'}, use_global_device_ids=true, to_apply=%region_3.4 | all-reduce | flops 128 | bytes 512 | tf_op jit(solution)/shard_map/psum | solution.py:12
  32.4 0.1 reshape.82
  32.5 1.5 %convolution_bitcast_fusion = f32[128,64]{1,0:T(8,128)} fusion(bf16[64,2]{0,1:T(2,128)(2,1)S(1)} %reshape.82, s32[128,2]{0,1:T(2,128)} %param.4), kind=kOutput, calls=%fused_computation.23 | convolution fusion | flops 33024 | bytes 34048
  34.0 0.2 reduce-scatter.7.cloned.1.call-start
  34.2 0.7 convert_bitcast_fusion.1
  34.9 3.8 %multiply_reduce_fusion = f32[128,2]{1,0:T(8,128)S(1)} fusion(bf16[128,2,4096]{2,1,0:T(2,128)(2,1)} %param.3), kind=kLoop, calls=%fused_computation.8 | loop fusion | flops 3145472 | bytes 2098176 | tf_op jit(solution)/shard_map/reduce_sum | solution.py:29
  38.9 33.4 %all-reduce.35.cloned.1.call-done = (bf16[1,32,2,4096]{3,2,1,0:T(2,128)(2,1)}, bf16[1,32,2,4096]{3,2,1,0:T(2,128)(2,1)}) async-done(((bf16[1,32,2,4096]{3,2,1,0:T(2,128)(2,1)}, bf16[1,32,2,4096]{3,2,1,0:T(2,128)(2,1)}), (bf16[1,32,2,4096]{3,2,1,0:T(2,128)(2,1)}, bf16[1,32,2,4096]{3,2,1,0:T(2,128)(2,1)})) %all-reduce.35.cloned.1.call-update) | async-done | bytes 1048592 | tf_op jit(solution)/shard_map/psum | solution.py:12
  72.3 1.5 constant_dynamic-update-slice_fusion.1
  73.7 1.5 %constant_dynamic-update-slice_fusion = bf16[2,32,2,4096]{3,2,1,0:T(2,128)(2,1)S(1)} fusion(bf16[2,32,2,4096]{3,2,1,0:T(2,128)(2,1)S(1)} %constant_dynamic-update-slice_fusion.1, bf16[1,32,2,4096]{3,2,1,0:T(2,128)(2,1)} %get-tuple-element.10), kind=kLoop, calls=%fused_computation.124 | loop fusion | bytes 1048576 | tf_op jit(solution)/shard_map/stack | solution.py:43
  75.3 1.2 multiply_reduce_fusion.1
  76.4 0.6 copy.44
  77.2 2.3 %fusion.62 = (bf16[8,64,2,4096]{3,1,2,0:T(8,128)(2,1)S(1)}, bf16[8,64,2,4096]{3,1,2,0:T(8,128)(2,1)}, bf16[8,64,2,4096]{3,1,2,0:T(8,128)(2,1)}) fusion(bf16[64,2,4096]{2,0,1:T(8,128)(2,1)S(1)} %bitcast.172), kind=kLoop, calls=%fused_computation.70 | loop fusion | bytes 4194304
  79.5 0.4 fusion.48
  79.9 0.4 fusion.50
  80.2 0.4 fusion.52
  80.6 0.4 fusion.54
  81.0 0.4 fusion.56
  81.4 0.4 fusion.58
  81.8 0.4 fusion.60
  82.2 0.1 multiply_divide_fusion
  82.3 2.4 %fusion.29 = f32[8,64,128]{2,1,0:T(8,128)S(1)} fusion(bf16[8,64,2,4096]{3,1,0,2:T(8,128)(2,1)S(1)} %fusion.60, bf16[128,2,4096,1]{2,1,0,3:T(2,128)(2,1)S(1)} %bitcast.188, f32[2,64,128]{2,1,0:T(8,128)S(1)} %multiply_divide_fusion), kind=kOutput, calls=%fused_computation.19 | convolution fusion | flops 1073938432 | bytes 10813440 | tf_op jit(solution)/shard_map/lsku,rku->klsr/dot_general | solution.py:57
  84.7 2.4 %fusion.64 = (bf16[8,64,2,4096]{3,1,2,0:T(8,128)(2,1)S(1)}, bf16[8,64,2,4096]{3,1,2,0:T(8,128)(2,1)}, bf16[8,64,2,4096]{3,1,2,0:T(8,128)(2,1)}) fusion(bf16[8,64,2,4096]{3,1,2,0:T(8,128)(2,1)S(1)} %get-tuple-element.32, bf16[64,2,4096]{2,0,1:T(8,128)(2,1)S(1)} %bitcast.180, bf16[8,64,2,4096]{3,1,2,0:T(8,128)(2,1)} %get-tuple-element.33, ...), kind=kLoop, calls=%fused_computation.72 | loop fusion | bytes 4194304
  87.1 2.2 %fusion.66 = (bf16[8,64,2,4096]{3,1,2,0:T(8,128)(2,1)S(1)}, bf16[8,64,2,4096]{3,1,2,0:T(8,128)(2,1)}, bf16[8,64,2,4096]{3,1,2,0:T(8,128)(2,1)}) fusion(bf16[8,64,2,4096]{3,1,2,0:T(8,128)(2,1)S(1)} %get-tuple-element.29, bf16[64,2,4096]{2,0,1:T(8,128)(2,1)S(1)} %bitcast.181, bf16[8,64,2,4096]{3,1,2,0:T(8,128)(2,1)} %get-tuple-element.30, ...), kind=kLoop, calls=%fused_computation.74 | loop fusion | bytes 4194304
  89.3 2.2 %fusion.68 = (bf16[8,64,2,4096]{3,1,2,0:T(8,128)(2,1)S(1)}, bf16[8,64,2,4096]{3,1,2,0:T(8,128)(2,1)}, bf16[8,64,2,4096]{3,1,2,0:T(8,128)(2,1)}) fusion(bf16[8,64,2,4096]{3,1,2,0:T(8,128)(2,1)S(1)} %get-tuple-element.26, bf16[64,2,4096]{2,0,1:T(8,128)(2,1)S(1)} %bitcast.182, bf16[8,64,2,4096]{3,1,2,0:T(8,128)(2,1)} %get-tuple-element.27, ...), kind=kLoop, calls=%fused_computation.76 | loop fusion | bytes 4194304
  91.4 2.2 %fusion.70 = (bf16[8,64,2,4096]{3,1,2,0:T(8,128)(2,1)S(1)}, bf16[8,64,2,4096]{3,1,2,0:T(8,128)(2,1)}, bf16[8,64,2,4096]{3,1,2,0:T(8,128)(2,1)}) fusion(bf16[8,64,2,4096]{3,1,2,0:T(8,128)(2,1)S(1)} %get-tuple-element.23, bf16[64,2,4096]{2,0,1:T(8,128)(2,1)S(1)} %bitcast.183, bf16[8,64,2,4096]{3,1,2,0:T(8,128)(2,1)} %get-tuple-element.24, ...), kind=kLoop, calls=%fused_computation.78 | loop fusion | bytes 4194304
  93.7 2.2 %fusion.72 = (bf16[8,64,2,4096]{3,1,2,0:T(8,128)(2,1)S(1)}, bf16[8,64,2,4096]{3,1,2,0:T(8,128)(2,1)}, bf16[8,64,2,4096]{3,1,2,0:T(8,128)(2,1)}) fusion(bf16[8,64,2,4096]{3,1,2,0:T(8,128)(2,1)S(1)} %get-tuple-element.20, bf16[64,2,4096]{2,0,1:T(8,128)(2,1)S(1)} %bitcast.184, bf16[8,64,2,4096]{3,1,2,0:T(8,128)(2,1)} %get-tuple-element.21, ...), kind=kLoop, calls=%fused_computation.80 | loop fusion | bytes 4194304
  95.9 2.2 %fusion.74 = (bf16[8,64,2,4096]{3,1,2,0:T(8,128)(2,1)S(1)}, bf16[8,64,2,4096]{3,1,2,0:T(8,128)(2,1)}, bf16[8,64,2,4096]{3,1,2,0:T(8,128)(2,1)}) fusion(bf16[8,64,2,4096]{3,1,2,0:T(8,128)(2,1)S(1)} %get-tuple-element.17, bf16[64,2,4096]{2,0,1:T(8,128)(2,1)S(1)} %bitcast.185, bf16[8,64,2,4096]{3,1,2,0:T(8,128)(2,1)} %get-tuple-element.18, ...), kind=kLoop, calls=%fused_computation.82 | loop fusion | bytes 4194304
  98.0 2.2 %fusion.76 = (bf16[8,64,2,4096]{3,1,2,0:T(8,128)(2,1)S(1)}, bf16[8,64,2,4096]{3,1,2,0:T(8,128)(2,1)}, bf16[8,64,2,4096]{3,1,2,0:T(8,128)(2,1)}) fusion(bf16[8,64,2,4096]{3,1,2,0:T(8,128)(2,1)S(1)} %get-tuple-element.14, bf16[64,2,4096]{2,0,1:T(8,128)(2,1)S(1)} %bitcast.186, bf16[8,64,2,4096]{3,1,2,0:T(8,128)(2,1)} %get-tuple-element.15, ...), kind=kLoop, calls=%fused_computation.84 | loop fusion | bytes 4194304 | tf_op jit(solution)/shard_map/stack | solution.py:20
  100.2 2.4 %fusion.42 = f32[8,64,128]{2,1,0:T(8,128)S(1)} fusion(bf16[128,2,4096,1]{2,1,0,3:T(2,128)(2,1)S(1)} %bitcast.189, bf16[8,64,2,4096]{3,1,2,0:T(8,128)(2,1)S(1)} %get-tuple-element.11, f32[2,64,128]{2,1,0:T(8,128)S(1)} %multiply_divide_fusion), kind=kOutput, calls=%fused_computation.22 | convolution fusion | flops 1073938432 | bytes 10813440 | tf_op jit(solution)/shard_map/lsku,rku->klsr/dot_general | solution.py:57
  102.7 1.0 slice-done.1
  103.7 2.4 %fusion.32 = f32[8,64,128]{2,1,0:T(8,128)S(1)} fusion(bf16[128,2,4096,1]{2,1,0,3:T(2,128)(2,1)S(1)} %bitcast.190, bf16[8,64,2,4096]{3,1,2,0:T(8,128)(2,1)S(1)} %bitcast.195, f32[2,64,128]{2,1,0:T(8,128)S(1)} %multiply_divide_fusion), kind=kOutput, calls=%fused_computation.20 | convolution fusion | flops 1073938432 | bytes 10813440 | tf_op jit(solution)/shard_map/lsku,rku->klsr/dot_general | solution.py:57
  106.1 6.2 %fusion.37 = f32[8,64,128]{2,1,0:T(8,128)S(1)} fusion(bf16[128,2,4096,1]{2,1,0,3:T(2,128)(2,1)S(1)} %bitcast.191, bf16[8,64,2,4096]{3,1,2,0:T(8,128)(2,1)} %get-tuple-element.13, f32[2,64,128]{2,1,0:T(8,128)S(1)} %multiply_divide_fusion), kind=kOutput, calls=%fused_computation.21 | convolution fusion | flops 1073938432 | bytes 10813440 | tf_op jit(solution)/shard_map/lsku,rku->klsr/dot_general | solution.py:57
  112.4 1.8 %copy.78 = f32[32,64,128]{1,0,2:T(8,128)S(1)} copy(f32[32,64,128]{2,1,0:T(8,128)S(1)} %pad_maximum_fusion) | data formatting | bytes 2097152
  114.2 1.6 %reshape.105 = f32[128,2048]{1,0:T(8,128)} reshape(f32[128,32,64]{2,1,0:T(8,128)S(1)} %bitcast.187) | data formatting | bytes 2097152
  115.9 0.8 copy.81
  116.8 18.8 %reduce-scatter.7.cloned.1.call-done = f32[64,2048]{1,0:T(8,128)} async-done(((f32[128,2048]{1,0:T(8,128)}), f32[64,2048]{1,0:T(8,128)}) %reduce-scatter.7.cloned.1.call-update) | async-done | bytes 524304
  135.6 1.5 reshape.106
  137.1 0.6 copy.79
  137.7 1.1 broadcast_divide_fusion
  (28 shorter events, 0.6 us)
Async XLA Ops:
  7.4 64.9 %all-reduce.35.cloned.1.call-start = ((), (), s32[]{:S(2)}) async-start(), calls=%async_computation.4 | async-start | bytes 2097152 | tf_op jit(solution)/shard_map/psum | solution.py:12
  17.1 98.8 %reduce-scatter.9.cloned.1.call-start = ((), (), s32[]{:S(2)}) async-start(), calls=%async_computation.3 | async-start | bytes 98304
  34.0 101.6 %reduce-scatter.7.cloned.1.call-start = ((), (), s32[]{:S(2)}) async-start(), calls=%async_computation.2 | async-start | bytes 1572864
  79.5 2.8 %copy-start = (bf16[128,2,4096]{2,1,0:T(2,128)(2,1)S(1)}, bf16[128,2,4096]{2,1,0:T(2,128)(2,1)}, u32[]{:S(2)}) copy-start(bf16[128,2,4096]{2,1,0:T(2,128)(2,1)} %param.3) | copy-start | bytes 6291460
  100.2 2.4 %slice-start = ((s8[8388608]{0:T(1024)(128)(4,1)}), s8[4194304]{0:T(1024)(128)(4,1)S(1)}, s32[]{:S(2)}) async-start(s8[8388608]{0:T(1024)(128)(4,1)} %bitcast.194), calls=%async_computation.5 | async-start | bytes 8388608
  100.2 3.5 %slice-start.1 = ((s8[8388608]{0:T(1024)(128)(4,1)}), s8[4194304]{0:T(1024)(128)(4,1)S(1)}, s32[]{:S(2)}) async-start(s8[8388608]{0:T(1024)(128)(4,1)} %bitcast.194), calls=%async_computation.6 | async-start | bytes 8388608
Sparse Core Ops, SparseCore 0:
  17.2 54.9 all-reduce.34
Sparse Core Ops, SparseCore 1:
  34.1 8.0 reduce-scatter.8
  116.0 19.6 reduce-scatter.6
where the time goes:
time: 147 us; the launch traced here: 146 us
  waiting for transfers between devices  52.3 us (36%)
  local copies, waits for them, and re-layouts  38.2 us (26%)
  between operations  16.4 us (11%)
  matrix products  15 us (10%)
  blocking collectives  13.6 us (9%)
  other arithmetic  10.5 us (7%)
    psum x1, waiting for transfers between devices, from_root(): return lax.psum(jnp.where(mine, array, jnp.zeros_like(array)), axis)  33.4 us
    unnamed x28, local copies, waits for them, and re-layouts  27.6 us
    unnamed x5, waiting for transfers between devices  18.9 us
    psum x1, blocking collectives, from_root(): return lax.psum(jnp.where(mine, array, jnp.zeros_like(array)), axis)  13.6 us
    dot_general x4, matrix products, body(): jnp.einsum('lsku,rku->klsr', lag_shifted, traces, preferred_element_type=...  13.5 us
    gather x1, local copies, waits for them, and re-layouts, body(): picked = traces[local_rows].reshape(panels_here, per_panel, seg_here, width)  4.25 us
    reduce_sum x1, other arithmetic, body(): jnp.mean(jnp.square(traces.astype(jnp.float32)), axis=2) + 1e-05  3.84 us
  transfers between devices with their start and end apart: 3, of which 2 were waited for; matrix products, arithmetic and copies ran while one was open for 35% of the time, Pallas kernels for 0%

commit v1 on v0

--- a/solution.py
+++ b/solution.py
@@ -9,7 +9,7 @@
 
 def from_root(array, axis, root):
     mine = lax.axis_index(axis) == root
-    return lax.psum(jnp.where(mine, array, jnp.zeros_like(array)), axis)
+    return jnp.sum(lax.all_gather(jnp.where(mine, array, jnp.zeros_like(array)), axis), axis=0)
 
 
 def shifted_block(src, first, count):

time: 147 us -> 196 us (1.33); the launches traced: 146 us -> 192 us
  waiting for transfers between devices: 52.3 us -> 79.9 us
  other arithmetic: 10.5 us -> 21.2 us
  blocking collectives: 13.6 us -> 20.3 us
    all_gather x0 -> x2, waiting for transfers between devices: none -> 61 us  [from_root(): lax.all_gather(jnp.where(mine, array, jnp.zeros_like(array)), axis)]
    psum x1 -> x0, waiting for transfers between devices: 33.4 us -> none  [from_root(): return lax.psum(jnp.where(mine, array, jnp.zeros_like(array)), axis)]
    all_gather x0 -> x2, blocking collectives: none -> 20.3 us  [from_root(): lax.all_gather(jnp.where(mine, array, jnp.zeros_like(array)), axis)]
    psum x1 -> x0, blocking collectives: 13.6 us -> none  [from_root(): return lax.psum(jnp.where(mine, array, jnp.zeros_like(array)), axis)]
    reduce_sum x0 -> x4, other arithmetic: none -> 9.26 us  [from_root(): jnp.sum(lax.all_gather(jnp.where(mine, array, jnp.zeros_like(array)), axi...]
    unnamed x28 -> x31, local copies, waits for them, and re-layouts: 27.6 us -> 29 us
    unnamed x5 -> x6, waiting for transfers between devices: 18.9 us -> 18.9 us
  transfers between devices with their start and end apart: 3 -> 4, of which waited for: 2 -> 3; matrix products, arithmetic and copies ran while one was open for 35% -> 32% of each run, Pallas kernels for 0% -> 0%
where the time goes in v1:
time: 196 us; the launch traced here: 192 us
  waiting for transfers between devices  79.9 us (41%)
  local copies, waits for them, and re-layouts  38.4 us (20%)
  other arithmetic  21.2 us (11%)
  blocking collectives  20.3 us (10%)
  between operations  16.7 us (9%)
  matrix products  15.1 us (8%)
    all_gather x2, waiting for transfers between devices, from_root(): lax.all_gather(jnp.where(mine, array, jnp.zeros_like(array)), axis)  61 us
    unnamed x31, local copies, waits for them, and re-layouts  29 us
    all_gather x2, blocking collectives, from_root(): lax.all_gather(jnp.where(mine, array, jnp.zeros_like(array)), axis)  20.3 us
    unnamed x6, waiting for transfers between devices  18.9 us
    dot_general x4, matrix products, body(): jnp.einsum('lsku,rku->klsr', lag_shifted, traces, preferred_element_type=...  13.6 us
    reduce_sum x4, other arithmetic, from_root(): jnp.sum(lax.all_gather(jnp.where(mine, array, jnp.zeros_like(array)), axi...  9.26 us
    gather x1, local copies, waits for them, and re-layouts, body(): picked = traces[local_rows].reshape(panels_here, per_panel, seg_here, width)  4.24 us
  transfers between devices with their start and end apart: 4, of which 3 were waited for; matrix products, arithmetic and copies ran while one was open for 32% of the time, Pallas kernels for 0%

profile of v1, /device:TPU:0, one launch (start us, length us, event | category | flops | bytes accessed | tf_op | source)
XLA Modules:
  0.0 192.2 jit_solution(5646884614282416637)
XLA Ops:
  7.4 0.8 multiply_reduce_fusion.2
  8.2 0.7 fusion.111
  10.2 0.8 broadcast_subtract_fusion
  11.1 4.2 %gather_fusion = bf16[64,2,4096]{2,1,0:T(2,128)(2,1)S(1)} fusion(bf16[128,2,4096]{2,1,0:T(2,128)(2,1)} %param.3, s32[1024]{0:T(1024)S(1)} %pad_clamp_fusion), kind=kCustom, calls=%fused_computation | custom fusion | bytes 2097408 | tf_op jit(solution)/shard_map/gather | solution.py:33
  15.3 1.8 broadcast_select_fusion.1
  17.2 0.7 all-gather.11.cloned.1.call-update
  18.0 0.8 copy.71
  18.8 0.6 gather_fusion.1
  19.6 12.6 %all-gather.4 = bf16[4,32,2]{1,2,0:T(2,128)(2,1)S(1)} all-gather(bf16[1,32,2]{1,2,0:T(2,128)(2,1)S(1)} %bitcast.208), channel_id=4, replica_groups=mesh['grp'=2,'chan'=4,'tm'=2,'sub'=2] {'chan'}, dimensions={0}, use_global_device_ids=true | all-gather | bytes 640 | tf_op jit(solution)/shard_map/all_gather | solution.py:12
  32.2 7.6 %all-gather.5 = bf16[4,32,2]{1,2,0:T(2,128)(2,1)S(1)} all-gather(bf16[1,32,2]{1,2,0:T(2,128)(2,1)S(1)} %bitcast.207), channel_id=5, replica_groups=mesh['grp'=2,'chan'=4,'tm'=2,'sub'=2] {'chan'}, dimensions={0}, use_global_device_ids=true | all-gather | bytes 640 | tf_op jit(solution)/shard_map/all_gather | solution.py:12
  40.0 1.5 convolution_bitcast_fusion
  41.5 0.5 reduce-scatter.7.cloned.1.call-start
  42.1 3.8 %multiply_reduce_fusion = f32[128,2]{1,0:T(8,128)S(1)} fusion(bf16[128,2,4096]{2,1,0:T(2,128)(2,1)} %param.3), kind=kLoop, calls=%fused_computation.8 | loop fusion | flops 3145472 | bytes 2098176 | tf_op jit(solution)/shard_map/reduce_sum | solution.py:29
  45.9 0.7 convert_bitcast_fusion.1
  46.7 19.3 %all-gather.9.cloned.1.call-done = bf16[128,2,4096]{2,1,0:T(2,128)(2,1)} async-done(((bf16[32,2,4096]{2,1,0:T(2,128)(2,1)}), bf16[128,2,4096]{2,1,0:T(2,128)(2,1)}) %all-gather.9.cloned.1.call-update) | async-done | bytes 2097168 | tf_op jit(solution)/shard_map/all_gather | solution.py:12
  66.0 4.6 %reduce_sum.102 = bf16[32,2,4096]{2,1,0:T(2,128)(2,1)S(1)} reduce(bf16[4,32,2,4096]{3,2,1,0:T(2,128)(2,1)} %bitcast.195, bf16[]{:T(256)} %constant.42.clone.1), dimensions={0}, to_apply=%region_0.0 | reduce | flops 786432 | bytes 2621442 | tf_op jit(solution)/shard_map/reduce_sum | solution.py:12
  70.6 41.6 %all-gather.11.cloned.1.call-done = bf16[128,2,4096]{2,1,0:T(2,128)(2,1)} async-done(((bf16[32,2,4096]{2,1,0:T(2,128)(2,1)}), bf16[128,2,4096]{2,1,0:T(2,128)(2,1)}) %all-gather.11.cloned.1.call-update) | async-done | bytes 2097168 | tf_op jit(solution)/shard_map/all_gather | solution.py:12
  112.2 4.6 %reduce_sum.103 = bf16[32,2,4096]{2,1,0:T(2,128)(2,1)S(1)} reduce(bf16[4,32,2,4096]{3,2,1,0:T(2,128)(2,1)} %bitcast.196, bf16[]{:T(256)} %constant.42.clone.1), dimensions={0}, to_apply=%region_1.2 | reduce | flops 786432 | bytes 2621442 | tf_op jit(solution)/shard_map/reduce_sum | solution.py:12
  116.9 2.6 %multiply_reduce_fusion.1 = (f32[2,32,2]{2,1,0:T(8,128)S(1)}, bf16[2,32,2,4096]{3,2,1,0:T(2,128)(2,1)S(1)}) fusion(bf16[1,32,2,4096]{3,2,1,0:T(2,128)(2,1)S(1)} %bitcast.198, bf16[1,32,2,4096]{3,2,1,0:T(2,128)(2,1)S(1)} %bitcast.197), kind=kLoop, calls=%fused_computation.9 | loop fusion | flops 2097024 | bytes 2097664 | tf_op jit(solution)/shard_map/reduce_sum | solution.py:47
  119.5 0.6 copy.62
  120.1 2.7 %fusion.62 = (bf16[8,64,2,4096]{3,1,2,0:T(8,128)(2,1)}, bf16[8,64,2,4096]{3,1,2,0:T(8,128)(2,1)}, bf16[8,64,2,4096]{3,1,2,0:T(8,128)(2,1)}) fusion(bf16[64,2,4096]{2,0,1:T(8,128)(2,1)S(1)} %bitcast.173), kind=kLoop, calls=%fused_computation.70 | loop fusion | bytes 4194304
  122.9 2.7 %fusion.64 = (bf16[8,64,2,4096]{3,1,2,0:T(8,128)(2,1)}, bf16[8,64,2,4096]{3,1,2,0:T(8,128)(2,1)}, bf16[8,64,2,4096]{3,1,2,0:T(8,128)(2,1)}) fusion(bf16[8,64,2,4096]{3,1,2,0:T(8,128)(2,1)} %get-tuple-element.30, bf16[64,2,4096]{2,0,1:T(8,128)(2,1)S(1)} %bitcast.174, bf16[8,64,2,4096]{3,1,2,0:T(8,128)(2,1)} %get-tuple-element.31, ...), kind=kLoop, calls=%fused_computation.72 | loop fusion | bytes 4194304
  125.6 2.7 %fusion.66 = (bf16[8,64,2,4096]{3,1,2,0:T(8,128)(2,1)}, bf16[8,64,2,4096]{3,1,2,0:T(8,128)(2,1)}, bf16[8,64,2,4096]{3,1,2,0:T(8,128)(2,1)}) fusion(bf16[8,64,2,4096]{3,1,2,0:T(8,128)(2,1)} %get-tuple-element.27, bf16[64,2,4096]{2,0,1:T(8,128)(2,1)S(1)} %bitcast.175, bf16[8,64,2,4096]{3,1,2,0:T(8,128)(2,1)} %get-tuple-element.28, ...), kind=kLoop, calls=%fused_computation.74 | loop fusion | bytes 4194304
  128.3 2.6 %fusion.68 = (bf16[8,64,2,4096]{3,1,2,0:T(8,128)(2,1)}, bf16[8,64,2,4096]{3,1,2,0:T(8,128)(2,1)}, bf16[8,64,2,4096]{3,1,2,0:T(8,128)(2,1)}) fusion(bf16[8,64,2,4096]{3,1,2,0:T(8,128)(2,1)} %get-tuple-element.24, bf16[64,2,4096]{2,0,1:T(8,128)(2,1)S(1)} %bitcast.176, bf16[8,64,2,4096]{3,1,2,0:T(8,128)(2,1)} %get-tuple-element.25, ...), kind=kLoop, calls=%fused_computation.76 | loop fusion | bytes 4194304
  130.9 2.6 %fusion.70 = (bf16[8,64,2,4096]{3,1,2,0:T(8,128)(2,1)}, bf16[8,64,2,4096]{3,1,2,0:T(8,128)(2,1)}, bf16[8,64,2,4096]{3,1,2,0:T(8,128)(2,1)}) fusion(bf16[8,64,2,4096]{3,1,2,0:T(8,128)(2,1)} %get-tuple-element.21, bf16[64,2,4096]{2,0,1:T(8,128)(2,1)S(1)} %bitcast.177, bf16[8,64,2,4096]{3,1,2,0:T(8,128)(2,1)} %get-tuple-element.22, ...), kind=kLoop, calls=%fused_computation.78 | loop fusion | bytes 4194304
  133.5 2.7 %fusion.72 = (bf16[8,64,2,4096]{3,1,2,0:T(8,128)(2,1)}, bf16[8,64,2,4096]{3,1,2,0:T(8,128)(2,1)}, bf16[8,64,2,4096]{3,1,2,0:T(8,128)(2,1)}) fusion(bf16[8,64,2,4096]{3,1,2,0:T(8,128)(2,1)} %get-tuple-element.18, bf16[64,2,4096]{2,0,1:T(8,128)(2,1)S(1)} %bitcast.178, bf16[8,64,2,4096]{3,1,2,0:T(8,128)(2,1)} %get-tuple-element.19, ...), kind=kLoop, calls=%fused_computation.80 | loop fusion | bytes 4194304
  136.2 2.7 %fusion.74 = (bf16[8,64,2,4096]{3,1,2,0:T(8,128)(2,1)}, bf16[8,64,2,4096]{3,1,2,0:T(8,128)(2,1)}, bf16[8,64,2,4096]{3,1,2,0:T(8,128)(2,1)}) fusion(bf16[8,64,2,4096]{3,1,2,0:T(8,128)(2,1)} %get-tuple-element.15, bf16[64,2,4096]{2,0,1:T(8,128)(2,1)S(1)} %bitcast.179, bf16[8,64,2,4096]{3,1,2,0:T(8,128)(2,1)} %get-tuple-element.16, ...), kind=kLoop, calls=%fused_computation.82 | loop fusion | bytes 4194304
  138.8 2.6 %fusion.76 = (bf16[8,64,2,4096]{3,1,2,0:T(8,128)(2,1)}, bf16[8,64,2,4096]{3,1,2,0:T(8,128)(2,1)}, bf16[8,64,2,4096]{3,1,2,0:T(8,128)(2,1)}) fusion(bf16[8,64,2,4096]{3,1,2,0:T(8,128)(2,1)} %get-tuple-element.12, bf16[64,2,4096]{2,0,1:T(8,128)(2,1)S(1)} %bitcast.180, bf16[8,64,2,4096]{3,1,2,0:T(8,128)(2,1)} %get-tuple-element.13, ...), kind=kLoop, calls=%fused_computation.84 | loop fusion | bytes 4194304 | tf_op jit(solution)/shard_map/stack | solution.py:20
  141.4 0.1 multiply_divide_fusion
  141.6 6.1 %fusion.42 = f32[8,64,128]{2,1,0:T(8,128)S(1)} fusion(bf16[128,2,4096,1]{2,1,0,3:T(2,128)(2,1)S(1)} %bitcast.190, bf16[8,64,2,4096]{3,1,2,0:T(8,128)(2,1)} %get-tuple-element.9, f32[2,64,128]{2,1,0:T(8,128)S(1)} %multiply_divide_fusion), kind=kOutput, calls=%fused_computation.22 | convolution fusion | flops 1073938432 | bytes 10813440 | tf_op jit(solution)/shard_map/lsku,rku->klsr/dot_general | solution.py:57
  147.7 2.7 %fusion.37 = f32[8,64,128]{2,1,0:T(8,128)S(1)} fusion(bf16[128,2,4096,1]{2,1,0,3:T(2,128)(2,1)S(1)} %bitcast.191, bf16[8,64,2,4096]{3,1,2,0:T(8,128)(2,1)S(1)} %bitcast.203, f32[2,64,128]{2,1,0:T(8,128)S(1)} %multiply_divide_fusion), kind=kOutput, calls=%fused_computation.21 | convolution fusion | flops 1073938432 | bytes 10813440 | tf_op jit(solution)/shard_map/lsku,rku->klsr/dot_general | solution.py:57
  150.4 0.7 slice-done.1
  151.1 2.4 %fusion.32 = f32[8,64,128]{2,1,0:T(8,128)S(1)} fusion(bf16[128,2,4096,1]{2,1,0,3:T(2,128)(2,1)S(1)} %bitcast.192, bf16[8,64,2,4096]{3,1,2,0:T(8,128)(2,1)S(1)} %bitcast.201, f32[2,64,128]{2,1,0:T(8,128)S(1)} %multiply_divide_fusion), kind=kOutput, calls=%fused_computation.20 | convolution fusion | flops 1073938432 | bytes 10813440 | tf_op jit(solution)/shard_map/lsku,rku->klsr/dot_general | solution.py:57
  153.6 0.4 fusion.48
  154.0 0.4 fusion.50
  154.4 0.4 fusion.52
  154.8 0.4 fusion.54
  155.2 0.4 fusion.56
  155.6 0.4 fusion.58
  155.9 0.4 fusion.60
  156.3 2.4 %fusion.29 = f32[8,64,128]{2,1,0:T(8,128)S(1)} fusion(bf16[8,64,2,4096]{3,1,0,2:T(8,128)(2,1)S(1)} %fusion.60, bf16[128,2,4096,1]{2,1,0,3:T(2,128)(2,1)S(1)} %bitcast.193, f32[2,64,128]{2,1,0:T(8,128)S(1)} %multiply_divide_fusion), kind=kOutput, calls=%fused_computation.19 | convolution fusion | flops 1073938432 | bytes 10813440 | tf_op jit(solution)/shard_map/lsku,rku->klsr/dot_general | solution.py:57
  158.8 1.8 copy.96
  160.7 1.6 reshape.111
  162.3 0.8 copy.99
  163.2 18.2 %reduce-scatter.7.cloned.1.call-done = f32[64,2048]{1,0:T(8,128)} async-done(((f32[128,2048]{1,0:T(8,128)}), f32[64,2048]{1,0:T(8,128)}) %reduce-scatter.7.cloned.1.call-update) | async-done | bytes 524304
  181.4 1.5 reshape.112
  182.8 0.6 copy.97
  183.5 1.1 broadcast_divide_fusion
  (39 shorter events, 1.0 us)
Async XLA Ops:
  7.4 58.6 %all-gather.9.cloned.1.call-start = ((), (), s32[]{:S(2)}) async-start(), calls=%async_computation.2 | async-start | bytes 2621440 | tf_op jit(solution)/shard_map/all_gather | solution.py:12
  17.2 95.1 %all-gather.11.cloned.1.call-start = ((), (), s32[]{:S(2)}) async-start(), calls=%async_computation.3 | async-start | bytes 2621440 | tf_op jit(solution)/shard_map/all_gather | solution.py:12
  17.9 144.4 %reduce-scatter.9.cloned.1.call-start = ((), (), s32[]{:S(2)}) async-start(), calls=%async_computation.5 | async-start | bytes 98304
  41.5 139.9 %reduce-scatter.7.cloned.1.call-start = ((), (), s32[]{:S(2)}) async-start(), calls=%async_computation.4 | async-start | bytes 1572864
  130.9 10.7 %copy-start = (bf16[128,2,4096]{2,1,0:T(2,128)(2,1)S(1)}, bf16[128,2,4096]{2,1,0:T(2,128)(2,1)}, u32[]{:S(2)}) copy-start(bf16[128,2,4096]{2,1,0:T(2,128)(2,1)} %param.3) | copy-start | bytes 6291460
  141.4 6.2 %slice-start.2 = ((s8[8388608]{0:T(1024)(128)(4,1)}), s8[4194304]{0:T(1024)(128)(4,1)S(1)}, s32[]{:S(2)}) async-start(s8[8388608]{0:T(1024)(128)(4,1)} %bitcast.202), calls=%async_computation.8 | async-start | bytes 8388608
  141.5 6.1 %slice-start.3 = ((s8[8388608]{0:T(1024)(128)(4,1)}), s8[4194304]{0:T(1024)(128)(4,1)S(1)}, s32[]{:S(2)}) async-start(s8[8388608]{0:T(1024)(128)(4,1)} %bitcast.202), calls=%async_computation.9 | async-start | bytes 8388608
  147.6 2.7 %slice-start = ((s8[8388608]{0:T(1024)(128)(4,1)}), s8[4194304]{0:T(1024)(128)(4,1)S(1)}, s32[]{:S(2)}) async-start(s8[8388608]{0:T(1024)(128)(4,1)} %bitcast.200), calls=%async_computation.6 | async-start | bytes 8388608
  147.7 3.4 %slice-start.1 = ((s8[8388608]{0:T(1024)(128)(4,1)}), s8[4194304]{0:T(1024)(128)(4,1)S(1)}, s32[]{:S(2)}) async-start(s8[8388608]{0:T(1024)(128)(4,1)} %bitcast.200), calls=%async_computation.7 | async-start | bytes 8388608
Sparse Core Ops, SparseCore 0:
  17.3 48.6 all-gather.8
  67.6 44.6 all-gather.10
Sparse Core Ops, SparseCore 1:
  41.6 9.4 reduce-scatter.8
  162.4 18.9 reduce-scatter.6
